TPU v7x, 32 devices: a whole 2x2x4 slice. The times are simulated.
32 devices in a mesh: dp: 8 (over z, y), mp: 4 (over x, core).
Axes of the slice: x: 2, y: 2, z: 4, core: 2. Of those that a mesh axis runs over, the one named last changes fastest.
Arguments:
- clean_latent: float32 [16, 768, 20], P('dp', 'mp'), may hold values from -6 to 6
- noise_draw: float32 [16, 768, 20], P('dp', 'mp'), may hold values from -6 to 6
- captions: bfloat16 [16, 256, 768], P('dp'), may hold values from -6 to 6
- caption_len: int32 [16], P('dp'), may hold values from 5 to 256, as said below
- timestep: int32 [16], P('dp'), may hold values from 0 to 999
- step_weight: float32 [1000], replicated, may hold values from 0.25 to 4
- step_count: int32 [1], replicated, may hold values from 2 to 20
- unit_slot: int32 [26], replicated, may hold values from 0 to 39, as said below
- master: float32 [40, 768, 768], P('dp', 'mp'), may hold values from -0.21875 to 0.21875
- first_moment: float32 [40, 768, 768], P('dp', 'mp'), may hold values from -8.34465e-07 to 8.34465e-07
- second_moment: float32 [40, 768, 768], P('dp', 'mp'), may hold values from 2.6031255e-16 to 1.0412502e-15
- latent_master: float32 [2, 20, 768], replicated, may hold values from -0.21875 to 0.21875
- latent_first: float32 [2, 20, 768], replicated, may hold values from -4.7683716e-06 to 4.7683716e-06
- latent_second: float32 [2, 20, 768], replicated, may hold values from 9.300595e-15 to 3.720238e-14
Outputs:
- updated_master: float32 [40, 768, 768], P('dp', 'mp')
- updated_first: float32 [40, 768, 768], P('dp', 'mp')
- updated_second: float32 [40, 768, 768], P('dp', 'mp')
- latent_updated: float32 [2, 20, 768], replicated
- latent_first_out: float32 [2, 20, 768], replicated
- latent_second_out: float32 [2, 20, 768], replicated
- grad_norm: float32 [], replicated
- loss_value: float32 [], replicated
Inputs may be any that keep to these rules, and one draw needn't show every extreme that they name: Clip b's caption occupies its first caption_len[b] token slots; some clip uses all 256. All entries differ, so every place holds at most one matrix; matrix u is owned by dp index unit_slot[u] // 5 in its place unit_slot[u] % 5; some dp index owns 5 matrices, every other index owns 0 to 5.
All inputs are finite; a program needn't handle non-finite values.
Results may differ from a plain program's by a relative error of at most 0.017.
Values may be sent and summed in bfloat16 or wider, within the bound.
No kernel may reach another device: no remote copies, remote signals or barrier semaphores. Data moves between devices by JAX's collectives and lax.ppermute only.
A program may use at most 192 MiB of HBM per device.

v0:
```python
import math
import jax
import jax.numpy as jnp
from jax import lax
from jax.sharding import PartitionSpec as P

D = 768
HD = 64
C = 20
FRAMES = 768
NT = 1000
UNITS = 26
highest = lax.Precision.HIGHEST
beta_first = 0.9
beta_second = 0.999
adam_epsilon = 1e-08
learn_rate = 0.02
decay_rate = 0.1
clip_limit = 0.002
norm_epsilon = 1e-06
masked_score = -1e30
bfloat = jnp.bfloat16
single = jnp.float32


def broadcast(array, axis, root):
    mine = lax.axis_index(axis) == root
    return lax.psum(jnp.where(mine, array, jnp.zeros_like(array)), axis)


def normed(values):
    center = values - jnp.mean(values, axis=-1, keepdims=True)
    spread_sq = jnp.mean(center * center, axis=-1, keepdims=True)
    return center * lax.rsqrt(spread_sq + norm_epsilon)


def modulate(values, shift, scale):
    return normed(values) * (1.0 + scale[:, None, :]) + shift[:, None, :]


def modulate_back(values, shift, scale, grad):
    _, pullback = jax.vjp(modulate, values, shift, scale)
    return pullback(grad)


def adamw(weight, moment, square, grad, count):
    moment = beta_first * moment + (1.0 - beta_first) * grad
    square = beta_second * square + (1.0 - beta_second) * grad * grad
    first_fix = 1.0 - jnp.power(beta_first, count)
    second_fix = 1.0 - jnp.power(beta_second, count)
    update = (
        moment / first_fix / (jnp.sqrt(square / second_fix) + adam_epsilon) + decay_rate * weight
    )
    return (weight - learn_rate * update, moment, square)


def sinusoid(timestep):
    half_width = D // 2
    frequency = jnp.exp(-math.log(10000.0) * jnp.arange(half_width).astype(single) / half_width)
    angles = timestep.astype(single)[:, None] * frequency[None, :]
    return jnp.concatenate([jnp.cos(angles), jnp.sin(angles)], axis=1)


def matmul(form, left, right):
    return jnp.einsum(form, left, right, preferred_element_type=single)


def masked_scores(query, keys, mask):
    scores = matmul("fhk,ghk->hfg", query, keys) * HD ** (-0.5)
    return jnp.where(mask[None, None, :], scores, masked_score)


def attend_forward(parts):
    query, keys, values, mask = parts
    scores = masked_scores(query, keys, mask)
    row_max = jnp.max(scores, axis=-1, keepdims=True)
    shifted = jnp.exp(scores - row_max)
    row_total = jnp.sum(shifted, axis=-1, keepdims=True)
    probs = shifted / row_total
    output = matmul("hfg,ghk->fhk", probs.astype(bfloat), values)
    return (output.astype(bfloat), (row_max + jnp.log(row_total))[..., 0])


def attend_backward(parts):
    query, keys, values, mask, grad_out, log_total = parts
    probs = jnp.exp(masked_scores(query, keys, mask) - log_total[..., None])
    grad_probs = matmul("fhk,ghk->hfg", grad_out, values)
    inner = jnp.sum(probs * grad_probs, axis=-1, keepdims=True)
    grad_scores = (probs * (grad_probs - inner)).astype(bfloat)
    grad_query = matmul("hfg,ghk->fhk", grad_scores, keys) * HD ** (-0.5)
    grad_keys = matmul("hfg,fhk->ghk", grad_scores, query) * HD ** (-0.5)
    grad_values = matmul("hfg,fhk->ghk", probs.astype(bfloat), grad_out)
    return (grad_query.astype(bfloat), grad_keys.astype(bfloat), grad_values.astype(bfloat))


def split_heads(values):
    return values.reshape(values.shape[0], values.shape[1], -1, HD)


def merge_heads(values):
    return values.reshape(values.shape[0], values.shape[1], -1)


def attention(query, keys, values, mask):
    output, log_total = lax.map(
        attend_forward, (split_heads(query), split_heads(keys), split_heads(values), mask)
    )
    return (merge_heads(output), log_total)


def attention_back(query, keys, values, mask, grad_out, log_total):
    grads = lax.map(
        attend_backward,
        (
            split_heads(query),
            split_heads(keys),
            split_heads(values),
            mask,
            split_heads(grad_out),
            log_total,
        ),
    )
    return tuple((merge_heads(item) for item in grads))


def spread(values):
    return lax.all_gather(values, "mp", axis=1, tiled=True)


def collect(values):
    return lax.psum_scatter(
        values.astype(jnp.bfloat16), "mp", scatter_dimension=1, tiled=True
    ).astype(jnp.float32)


def side_by_side(stack):
    return jnp.transpose(stack, (1, 0, 2)).reshape(stack.shape[1], -1)


def body(
    clean_latent,
    noise_draw,
    captions,
    caption_len,
    timestep,
    step_weight,
    step_count,
    unit_slot,
    master,
    first_moment,
    second_moment,
    latent_master,
    latent_first,
    latent_second,
):
    slots = master.shape[0]
    owner = unit_slot // slots
    place = unit_slot % slots

    def fetch_one(running, index):
        local = lax.dynamic_index_in_dim(master, place[index], 0, keepdims=False).astype(bfloat)
        return (running, broadcast(local, "dp", owner[index]))

    _, fetched = lax.scan(fetch_one, 0, jnp.arange(UNITS))
    weights = jnp.swapaxes(fetched, 1, 2)
    width = weights.shape[2]
    table = jnp.arange(step_weight.shape[0])
    clip_weight = jnp.sum(
        jnp.where(timestep[:, None] == table[None, :], step_weight[None, :], 0.0), axis=1
    )
    weight_total = lax.psum(jnp.sum(clip_weight), "dp")
    level = (timestep.astype(single) + 0.5) / NT
    noisy = (1.0 - level)[:, None, None] * clean_latent + level[:, None, None] * noise_draw
    target = noise_draw - clean_latent
    cap_mask = jnp.arange(captions.shape[1])[None, :] < caption_len[:, None]
    pooled = (
        jnp.sum(jnp.where(cap_mask[:, :, None], captions.astype(single), 0.0), axis=1)
        / caption_len.astype(single)[:, None]
    )
    sinus_low = sinusoid(timestep).astype(bfloat)
    pooled_low = pooled.astype(bfloat)
    cond_part = matmul("bd,de->be", sinus_low, weights[24]) + matmul(
        "bd,de->be", pooled_low, weights[25]
    )
    cond = lax.all_gather(cond_part, "mp", axis=1, tiled=True)
    active = jax.nn.silu(cond).astype(bfloat)
    modulation = lax.all_gather(
        matmul("bd,jde->bje", active, weights[16:24]), "mp", axis=2, tiled=True
    )
    hidden_zero = jnp.einsum("bfc,cd->bfd", noisy, latent_master[0], precision=highest)
    w_attn = side_by_side(weights[0:3])
    first_in = spread(modulate(hidden_zero, modulation[:, 0], modulation[:, 1]).astype(bfloat))
    self_proj = matmul("bfd,de->bfe", first_in, w_attn).astype(bfloat)
    self_query, self_keys, self_values = jnp.split(self_proj, 3, axis=2)
    self_mask = jnp.ones((self_query.shape[0], self_query.shape[1]), bool)
    self_flat, self_total = attention(self_query, self_keys, self_values, self_mask)
    self_branch = collect(matmul("bfk,dk->bfd", self_flat, weights[3]))
    hidden_one = hidden_zero + modulation[:, 2, None, :] * self_branch
    second_in = spread(normed(hidden_one).astype(bfloat))
    cross_query = matmul("bfd,de->bfe", second_in, weights[4]).astype(bfloat)
    w_text = side_by_side(weights[5:7])
    cross_keys, cross_values = jnp.split(
        matmul("bld,de->ble", captions, w_text).astype(bfloat), 2, axis=2
    )
    cross_flat, cross_total = attention(cross_query, cross_keys, cross_values, cap_mask)
    cross_branch = collect(matmul("bfk,dk->bfd", cross_flat, weights[7]))
    hidden_two = hidden_one + cross_branch
    w_up = side_by_side(weights[8:12])
    w_down = side_by_side(weights[12:16])
    third_in = spread(modulate(hidden_two, modulation[:, 3], modulation[:, 4]).astype(bfloat))
    upper_wide = matmul("bfd,dk->bfk", third_in, w_up).astype(bfloat).astype(single)
    activated = jax.nn.gelu(upper_wide, approximate=True).astype(bfloat)
    mlp_branch = collect(matmul("bfk,dk->bfd", activated, w_down))
    hidden_three = hidden_two + modulation[:, 5, None, :] * mlp_branch
    final_wide = (
        modulate(hidden_three, modulation[:, 6], modulation[:, 7]).astype(bfloat).astype(single)
    )
    predicted = jnp.einsum("bfd,cd->bfc", final_wide, latent_master[1], precision=highest)
    error = predicted - target
    loss_local = jnp.sum(clip_weight[:, None, None] * error * error)
    grad_pred = 2.0 / (C * FRAMES) * clip_weight[:, None, None] * error / weight_total
    grad_out_proj = jnp.einsum("bfc,bfd->cd", grad_pred, final_wide, precision=highest)
    grad_final = jnp.einsum("bfc,cd->bfd", grad_pred, latent_master[1], precision=highest)
    grad_three, shift_f, scale_f = modulate_back(
        hidden_three, modulation[:, 6], modulation[:, 7], grad_final
    )
    gate_m_grad = jnp.sum(grad_three * mlp_branch, axis=1)
    grad_mlp = spread((modulation[:, 5, None, :] * grad_three).astype(bfloat))
    grad_act = matmul("bfd,dk->bfk", grad_mlp, w_down)
    grad_w_down = matmul("bfd,bfk->dk", grad_mlp, activated)
    _, gelu_back = jax.vjp(lambda inner_in: jax.nn.gelu(inner_in, approximate=True), upper_wide)
    grad_upper = gelu_back(grad_act)[0].astype(bfloat)
    grad_w_up = matmul("bfd,bfk->dk", third_in, grad_upper)
    grad_third = collect(matmul("bfk,dk->bfd", grad_upper, w_up))
    grad_two, shift_m, scale_m = modulate_back(
        hidden_two, modulation[:, 3], modulation[:, 4], grad_third
    )
    grad_two = grad_two + grad_three
    grad_cross = spread(grad_two.astype(bfloat))
    grad_cross_flat = matmul("bfd,dk->bfk", grad_cross, weights[7]).astype(bfloat)
    grad_w_cross_out = matmul("bfd,bfk->dk", grad_cross, cross_flat)
    cq_grad, ck_grad, cv_grad = attention_back(
        cross_query, cross_keys, cross_values, cap_mask, grad_cross_flat, cross_total
    )
    grad_w_cq = matmul("bfd,bfk->dk", second_in, cq_grad)
    grad_w_text = matmul("bld,ble->de", captions, jnp.concatenate([ck_grad, cv_grad], axis=2))
    grad_second = collect(matmul("bfk,dk->bfd", cq_grad, weights[4]))
    _, norm_back = jax.vjp(normed, hidden_one)
    grad_one = grad_two + norm_back(grad_second)[0]
    gate_a_grad = jnp.sum(grad_one * self_branch, axis=1)
    grad_self = spread((modulation[:, 2, None, :] * grad_one).astype(bfloat))
    grad_self_flat = matmul("bfd,dk->bfk", grad_self, weights[3]).astype(bfloat)
    grad_w_self_out = matmul("bfd,bfk->dk", grad_self, self_flat)
    sq_grad, sk_grad, sv_grad = attention_back(
        self_query, self_keys, self_values, self_mask, grad_self_flat, self_total
    )
    grad_proj = jnp.concatenate([sq_grad, sk_grad, sv_grad], axis=2)
    grad_w_attn = matmul("bfd,bfe->de", first_in, grad_proj)
    grad_first = collect(matmul("bfe,de->bfd", grad_proj, w_attn))
    grad_zero, shift_a, scale_a = modulate_back(
        hidden_zero, modulation[:, 0], modulation[:, 1], grad_first
    )
    grad_zero = grad_zero + grad_one
    grad_in_proj = jnp.einsum("bfc,bfd->cd", noisy, grad_zero, precision=highest)
    grad_mod = jnp.stack(
        [shift_a, scale_a, gate_a_grad, shift_m, scale_m, gate_m_grad, shift_f, scale_f], axis=1
    )
    mod_own = (
        lax.psum_scatter(grad_mod.astype(jnp.bfloat16), "mp", scatter_dimension=2, tiled=True)
        .astype(jnp.float32)
        .astype(bfloat)
    )
    grad_ada = matmul("bd,bje->jde", active, mod_own)
    grad_active = matmul("bje,jde->bd", mod_own, weights[16:24])
    _, silu_back = jax.vjp(jax.nn.silu, cond)
    cond_own = lax.psum_scatter(
        silu_back(grad_active)[0], "mp", scatter_dimension=1, tiled=True
    ).astype(bfloat)
    grad_time = matmul("bd,be->de", sinus_low, cond_own)
    grad_pool = matmul("bd,be->de", pooled_low, cond_own)

    def columns(matrix, count):
        return jnp.transpose(matrix.reshape(matrix.shape[0], count, width), (1, 0, 2))

    grads_cols = jnp.concatenate(
        [
            columns(grad_w_attn, 3),
            grad_w_self_out[None],
            grad_w_cq[None],
            columns(grad_w_text, 2),
            grad_w_cross_out[None],
            columns(grad_w_up, 4),
            columns(grad_w_down, 4),
            grad_ada,
            grad_time[None],
            grad_pool[None],
        ],
        axis=0,
    )
    grads = jnp.swapaxes(grads_cols, 1, 2)
    local_ids = lax.axis_index("dp") * slots + jnp.arange(slots)
    pick = (unit_slot[None, :] == local_ids[:, None]).astype(single)
    live_slot = jnp.sum(pick, axis=1) > 0.5
    summed = lax.psum(grads, "dp")
    owned = jnp.einsum("su,ude->sde", pick, summed, precision=highest)
    latent_grad, loss_sum = lax.psum(
        (jnp.stack([grad_in_proj, grad_out_proj]), loss_local), ("dp", "mp")
    )
    square_sum = lax.psum(jnp.sum(owned * owned), ("dp", "mp")) + jnp.sum(latent_grad * latent_grad)
    grad_norm = jnp.sqrt(square_sum)
    factor = clip_limit / jnp.maximum(grad_norm, clip_limit)
    count = step_count[0].astype(single)
    new_weight, new_moment, new_square = adamw(
        master, first_moment, second_moment, owned * factor, count
    )
    keep = live_slot[:, None, None]
    latent_weight, latent_moment, latent_square = adamw(
        latent_master, latent_first, latent_second, latent_grad * factor, count
    )
    loss_value = loss_sum / (C * FRAMES * weight_total)
    return (
        jnp.where(keep, new_weight, master),
        jnp.where(keep, new_moment, first_moment),
        jnp.where(keep, new_square, second_moment),
        latent_weight,
        latent_moment,
        latent_square,
        grad_norm,
        loss_value,
    )


def solution(mesh):
    placed = (
        P("dp", "mp", None),
        P("dp", "mp", None),
        P("dp", None, None),
        P("dp"),
        P("dp"),
        P(),
        P(),
        P(),
        P("dp", "mp", None),
        P("dp", "mp", None),
        P("dp", "mp", None),
        P(),
        P(),
        P(),
    )
    return jax.shard_map(
        body,
        mesh=mesh,
        in_specs=placed,
        out_specs=(
            P("dp", "mp", None),
            P("dp", "mp", None),
            P("dp", "mp", None),
            P(),
            P(),
            P(),
            P(),
            P(),
        ),
        check_vma=False,
    )
```

profile of v0, /device:TPU:0, one launch (start us, length us, event | category | flops | bytes accessed | tf_op | source)
XLA Modules:
  0.0 3431.0 jit_solution(15511548824490936030)
XLA Ops:
  17.4 2054.4 %while.62 = (s32[]{:T(128)}, bf16[26,192,768]{2,1,0:T(8,128)(2,1)}, s32[26]{0:T(128)S(1)}, s32[26]{0:T(128)S(1)}, s32[26]{0:T(128)S(1)}, /*index=5*/bf16[5,192,7...) while((s32[]{:T(128)}, bf16[26,192,768]{2,1,0:T(8,128)(2,1)}, ...), condition=%wide.region_5.6_spmd, body=%wide.region_3.5_spmd.sunk | while | flops 294924 | bytes 2949439 | solution.py:164
  24.6 73.7 %all-reduce.9.cloned.1.call-done = bf16[1,192,768]{2,1,0:T(8,128)(2,1)} async-done(((bf16[1,192,768]{2,1,0:T(8,128)(2,1)}), bf16[1,192,768]{2,1,0:T(8,128)(2,1)}) %all-reduce.9.cloned.1.call-update) | async-done | bytes 294928 | tf_op jit(solution)/shard_map/while/body/eval_jaxpr/psum | solution.py:28
  107.0 70.1 %all-reduce.9.cloned.1.call-done = bf16[1,192,768]{2,1,0:T(8,128)(2,1)} async-done(((bf16[1,192,768]{2,1,0:T(8,128)(2,1)}), bf16[1,192,768]{2,1,0:T(8,128)(2,1)}) %all-reduce.9.cloned.1.call-update) | async-done | bytes 294928 | tf_op jit(solution)/shard_map/while/body/eval_jaxpr/psum | solution.py:28
  185.9 70.1 %all-reduce.9.cloned.1.call-done = bf16[1,192,768]{2,1,0:T(8,128)(2,1)} async-done(((bf16[1,192,768]{2,1,0:T(8,128)(2,1)}), bf16[1,192,768]{2,1,0:T(8,128)(2,1)}) %all-reduce.9.cloned.1.call-update) | async-done | bytes 294928 | tf_op jit(solution)/shard_map/while/body/eval_jaxpr/psum | solution.py:28
  264.7 70.1 %all-reduce.9.cloned.1.call-done = bf16[1,192,768]{2,1,0:T(8,128)(2,1)} async-done(((bf16[1,192,768]{2,1,0:T(8,128)(2,1)}), bf16[1,192,768]{2,1,0:T(8,128)(2,1)}) %all-reduce.9.cloned.1.call-update) | async-done | bytes 294928 | tf_op jit(solution)/shard_map/while/body/eval_jaxpr/psum | solution.py:28
  343.6 70.1 %all-reduce.9.cloned.1.call-done = bf16[1,192,768]{2,1,0:T(8,128)(2,1)} async-done(((bf16[1,192,768]{2,1,0:T(8,128)(2,1)}), bf16[1,192,768]{2,1,0:T(8,128)(2,1)}) %all-reduce.9.cloned.1.call-update) | async-done | bytes 294928 | tf_op jit(solution)/shard_map/while/body/eval_jaxpr/psum | solution.py:28
  422.5 70.1 %all-reduce.9.cloned.1.call-done = bf16[1,192,768]{2,1,0:T(8,128)(2,1)} async-done(((bf16[1,192,768]{2,1,0:T(8,128)(2,1)}), bf16[1,192,768]{2,1,0:T(8,128)(2,1)}) %all-reduce.9.cloned.1.call-update) | async-done | bytes 294928 | tf_op jit(solution)/shard_map/while/body/eval_jaxpr/psum | solution.py:28
  501.3 70.1 %all-reduce.9.cloned.1.call-done = bf16[1,192,768]{2,1,0:T(8,128)(2,1)} async-done(((bf16[1,192,768]{2,1,0:T(8,128)(2,1)}), bf16[1,192,768]{2,1,0:T(8,128)(2,1)}) %all-reduce.9.cloned.1.call-update) | async-done | bytes 294928 | tf_op jit(solution)/shard_map/while/body/eval_jaxpr/psum | solution.py:28
  580.2 70.1 %all-reduce.9.cloned.1.call-done = bf16[1,192,768]{2,1,0:T(8,128)(2,1)} async-done(((bf16[1,192,768]{2,1,0:T(8,128)(2,1)}), bf16[1,192,768]{2,1,0:T(8,128)(2,1)}) %all-reduce.9.cloned.1.call-update) | async-done | bytes 294928 | tf_op jit(solution)/shard_map/while/body/eval_jaxpr/psum | solution.py:28
  659.1 70.1 %all-reduce.9.cloned.1.call-done = bf16[1,192,768]{2,1,0:T(8,128)(2,1)} async-done(((bf16[1,192,768]{2,1,0:T(8,128)(2,1)}), bf16[1,192,768]{2,1,0:T(8,128)(2,1)}) %all-reduce.9.cloned.1.call-update) | async-done | bytes 294928 | tf_op jit(solution)/shard_map/while/body/eval_jaxpr/psum | solution.py:28
  738.0 70.1 %all-reduce.9.cloned.1.call-done = bf16[1,192,768]{2,1,0:T(8,128)(2,1)} async-done(((bf16[1,192,768]{2,1,0:T(8,128)(2,1)}), bf16[1,192,768]{2,1,0:T(8,128)(2,1)}) %all-reduce.9.cloned.1.call-update) | async-done | bytes 294928 | tf_op jit(solution)/shard_map/while/body/eval_jaxpr/psum | solution.py:28
  816.9 70.1 %all-reduce.9.cloned.1.call-done = bf16[1,192,768]{2,1,0:T(8,128)(2,1)} async-done(((bf16[1,192,768]{2,1,0:T(8,128)(2,1)}), bf16[1,192,768]{2,1,0:T(8,128)(2,1)}) %all-reduce.9.cloned.1.call-update) | async-done | bytes 294928 | tf_op jit(solution)/shard_map/while/body/eval_jaxpr/psum | solution.py:28
  895.7 70.1 %all-reduce.9.cloned.1.call-done = bf16[1,192,768]{2,1,0:T(8,128)(2,1)} async-done(((bf16[1,192,768]{2,1,0:T(8,128)(2,1)}), bf16[1,192,768]{2,1,0:T(8,128)(2,1)}) %all-reduce.9.cloned.1.call-update) | async-done | bytes 294928 | tf_op jit(solution)/shard_map/while/body/eval_jaxpr/psum | solution.py:28
  974.6 70.1 %all-reduce.9.cloned.1.call-done = bf16[1,192,768]{2,1,0:T(8,128)(2,1)} async-done(((bf16[1,192,768]{2,1,0:T(8,128)(2,1)}), bf16[1,192,768]{2,1,0:T(8,128)(2,1)}) %all-reduce.9.cloned.1.call-update) | async-done | bytes 294928 | tf_op jit(solution)/shard_map/while/body/eval_jaxpr/psum | solution.py:28
  1053.4 70.1 %all-reduce.9.cloned.1.call-done = bf16[1,192,768]{2,1,0:T(8,128)(2,1)} async-done(((bf16[1,192,768]{2,1,0:T(8,128)(2,1)}), bf16[1,192,768]{2,1,0:T(8,128)(2,1)}) %all-reduce.9.cloned.1.call-update) | async-done | bytes 294928 | tf_op jit(solution)/shard_map/while/body/eval_jaxpr/psum | solution.py:28
  1132.3 70.1 %all-reduce.9.cloned.1.call-done = bf16[1,192,768]{2,1,0:T(8,128)(2,1)} async-done(((bf16[1,192,768]{2,1,0:T(8,128)(2,1)}), bf16[1,192,768]{2,1,0:T(8,128)(2,1)}) %all-reduce.9.cloned.1.call-update) | async-done | bytes 294928 | tf_op jit(solution)/shard_map/while/body/eval_jaxpr/psum | solution.py:28
  1211.2 70.1 %all-reduce.9.cloned.1.call-done = bf16[1,192,768]{2,1,0:T(8,128)(2,1)} async-done(((bf16[1,192,768]{2,1,0:T(8,128)(2,1)}), bf16[1,192,768]{2,1,0:T(8,128)(2,1)}) %all-reduce.9.cloned.1.call-update) | async-done | bytes 294928 | tf_op jit(solution)/shard_map/while/body/eval_jaxpr/psum | solution.py:28
  1290.1 70.1 %all-reduce.9.cloned.1.call-done = bf16[1,192,768]{2,1,0:T(8,128)(2,1)} async-done(((bf16[1,192,768]{2,1,0:T(8,128)(2,1)}), bf16[1,192,768]{2,1,0:T(8,128)(2,1)}) %all-reduce.9.cloned.1.call-update) | async-done | bytes 294928 | tf_op jit(solution)/shard_map/while/body/eval_jaxpr/psum | solution.py:28
  1369.0 70.1 %all-reduce.9.cloned.1.call-done = bf16[1,192,768]{2,1,0:T(8,128)(2,1)} async-done(((bf16[1,192,768]{2,1,0:T(8,128)(2,1)}), bf16[1,192,768]{2,1,0:T(8,128)(2,1)}) %all-reduce.9.cloned.1.call-update) | async-done | bytes 294928 | tf_op jit(solution)/shard_map/while/body/eval_jaxpr/psum | solution.py:28
  1447.9 70.1 %all-reduce.9.cloned.1.call-done = bf16[1,192,768]{2,1,0:T(8,128)(2,1)} async-done(((bf16[1,192,768]{2,1,0:T(8,128)(2,1)}), bf16[1,192,768]{2,1,0:T(8,128)(2,1)}) %all-reduce.9.cloned.1.call-update) | async-done | bytes 294928 | tf_op jit(solution)/shard_map/while/body/eval_jaxpr/psum | solution.py:28
  1526.7 70.1 %all-reduce.9.cloned.1.call-done = bf16[1,192,768]{2,1,0:T(8,128)(2,1)} async-done(((bf16[1,192,768]{2,1,0:T(8,128)(2,1)}), bf16[1,192,768]{2,1,0:T(8,128)(2,1)}) %all-reduce.9.cloned.1.call-update) | async-done | bytes 294928 | tf_op jit(solution)/shard_map/while/body/eval_jaxpr/psum | solution.py:28
  1605.6 70.1 %all-reduce.9.cloned.1.call-done = bf16[1,192,768]{2,1,0:T(8,128)(2,1)} async-done(((bf16[1,192,768]{2,1,0:T(8,128)(2,1)}), bf16[1,192,768]{2,1,0:T(8,128)(2,1)}) %all-reduce.9.cloned.1.call-update) | async-done | bytes 294928 | tf_op jit(solution)/shard_map/while/body/eval_jaxpr/psum | solution.py:28
  1684.5 70.1 %all-reduce.9.cloned.1.call-done = bf16[1,192,768]{2,1,0:T(8,128)(2,1)} async-done(((bf16[1,192,768]{2,1,0:T(8,128)(2,1)}), bf16[1,192,768]{2,1,0:T(8,128)(2,1)}) %all-reduce.9.cloned.1.call-update) | async-done | bytes 294928 | tf_op jit(solution)/shard_map/while/body/eval_jaxpr/psum | solution.py:28
  1763.4 70.1 %all-reduce.9.cloned.1.call-done = bf16[1,192,768]{2,1,0:T(8,128)(2,1)} async-done(((bf16[1,192,768]{2,1,0:T(8,128)(2,1)}), bf16[1,192,768]{2,1,0:T(8,128)(2,1)}) %all-reduce.9.cloned.1.call-update) | async-done | bytes 294928 | tf_op jit(solution)/shard_map/while/body/eval_jaxpr/psum | solution.py:28
  1842.2 70.1 %all-reduce.9.cloned.1.call-done = bf16[1,192,768]{2,1,0:T(8,128)(2,1)} async-done(((bf16[1,192,768]{2,1,0:T(8,128)(2,1)}), bf16[1,192,768]{2,1,0:T(8,128)(2,1)}) %all-reduce.9.cloned.1.call-update) | async-done | bytes 294928 | tf_op jit(solution)/shard_map/while/body/eval_jaxpr/psum | solution.py:28
  1921.1 70.1 %all-reduce.9.cloned.1.call-done = bf16[1,192,768]{2,1,0:T(8,128)(2,1)} async-done(((bf16[1,192,768]{2,1,0:T(8,128)(2,1)}), bf16[1,192,768]{2,1,0:T(8,128)(2,1)}) %all-reduce.9.cloned.1.call-update) | async-done | bytes 294928 | tf_op jit(solution)/shard_map/while/body/eval_jaxpr/psum | solution.py:28
  2000.0 70.1 %all-reduce.9.cloned.1.call-done = bf16[1,192,768]{2,1,0:T(8,128)(2,1)} async-done(((bf16[1,192,768]{2,1,0:T(8,128)(2,1)}), bf16[1,192,768]{2,1,0:T(8,128)(2,1)}) %all-reduce.9.cloned.1.call-update) | async-done | bytes 294928 | tf_op jit(solution)/shard_map/while/body/eval_jaxpr/psum | solution.py:28
  2074.1 5.2 all-gather
  2082.0 8.7 all_gather.25
  2090.7 7.2 fusion.215
  2101.1 21.8 all-gather.8.cloned.1.call-done
  2127.2 9.4 while.63
  2141.8 31.5 reduce-scatter.13.cloned.1.call-done
  2177.7 22.3 all-gather.10.cloned.1.call-done
  2203.5 5.6 while.64
  2209.1 3.7 convolution_convert_fusion.6
  2216.1 29.8 reduce-scatter.15.cloned.1.call-done
  2253.0 20.8 all-gather.12.cloned.1.call-done
  2273.8 4.1 convolution_convert_fusion.5
  2279.3 4.5 convolution_convert_fusion.4
  2285.3 22.4 psum.42
  2326.2 24.0 all-gather.14.cloned.1.call-done
  2350.2 7.3 fusion.115
  2362.3 33.0 reduce-scatter.19.cloned.1.call-done
  2402.9 23.8 all-gather.16.cloned.1.call-done
  2431.0 14.6 while.65
  2449.1 33.0 reduce-scatter.21.cloned.1.call-done
  2490.4 24.0 all-gather.18.cloned.1.call-done
  2519.5 30.1 while.66
  2522.0 4.5 multiply_reduce_fusion.16
  2526.5 4.5 multiply_convert_fusion.8
  2537.0 4.5 multiply_reduce_fusion.16
  2541.6 4.5 multiply_convert_fusion.8
  2549.6 4.9 convolution_convert_fusion.1
  2557.6 4.6 fusion.218
  2565.2 5.2 copy_bitcast_fusion
  2597.3 18.7 reduce-scatter.25.cloned.1.call-done
  2623.9 17.1 reduce-scatter.27.cloned.1.call-done
  2646.2 46.0 %concatenate.16 = f32[26,768,192]{1,0,2:T(8,128)} concatenate(f32[3,768,192]{1,0,2:T(4,128)S(1)} %bitcast.450, f32[1,768,192]{1,0,2:T(1,128)} %copy.315, f32[1,768,192]{1,0,2:T(1,128)} %copy.316, f32[2,768,192]{1,0,2:T(2,128)S(1)} %bitcast.466, f32[1,768,192]{1,0,2:T(1,128)} %copy.317, f32[4,768,192]{1,0,2:T(4,128)} %get-tuple-element.415, f32[4,768,192]{1,0,2:T(4,128)} %get-tuple-element.414, ...), dimensions={0} | concatenate | bytes 30670848 | tf_op jit(solution)/shard_map/concatenate | solution.py:285
  2693.8 73.2 %all-reduce.7.cloned.1.call-done = f32[2,20,768]{2,1,0:T(8,128)} async-done(((f32[2,20,768]{2,1,0:T(8,128)}), f32[2,20,768]{2,1,0:T(8,128)}) %all-reduce.7.cloned.1.call-update) | async-done | bytes 122896 | tf_op jit(solution)/shard_map/psum | solution.py:306
  2768.6 571.5 %all-reduce.5.cloned.1.call-done = f32[26,192,768]{2,0,1:T(8,128)} async-done(((f32[26,192,768]{2,0,1:T(8,128)}), f32[26,192,768]{2,0,1:T(8,128)}) %all-reduce.5.cloned.1.call-update) | async-done | bytes 15335440 | tf_op jit(solution)/shard_map/psum | solution.py:304
  3340.1 12.6 multiply_reduce_fusion.3
  3352.7 39.8 %all-reduce = (f32[]{:T(128)}, f32[]{:T(128)}) all-reduce(f32[]{:T(128)} %get-tuple-element.410, f32[]{:T(128)} %get-tuple-element.412), channel_id=1, replica_groups=mesh['dp'=8,'mp'=4] {'dp','mp'}, use_global_device_ids=true, to_apply=%region_54.55 | all-reduce | flops 2 | bytes 16 | tf_op jit(solution)/shard_map/psum | solution.py:309
  3397.2 15.7 copy_select_fusion
  (675 shorter events, 308.4 us)
Async XLA Ops:
  8.7 2064.3 %copy-start.110 = (f32[2]{0:T(128)}, f32[2]{0:T(128)S(1)}, u32[]{:S(2)}) copy-start(f32[2]{0:T(128)S(1)} %convert_element_type.199) | copy-start | bytes 28
  14.5 2158.8 %copy-start = (f32[2,192,768]{2,1,0:T(8,128)}, f32[2,192,768]{2,1,0:T(8,128)S(1)}, u32[]{:S(2)}) copy-start(f32[2,192,768]{2,1,0:T(8,128)S(1)} %get-tuple-element.408) | copy-start | bytes 3538948
  14.5 2084.2 %copy-start.75 = (f32[2,192]{1,0:T(2,128)}, f32[2,192]{1,0:T(2,128)S(1)}, u32[]{:S(2)}) copy-start(f32[2,192]{1,0:T(2,128)S(1)} %broadcast_multiply_fusion.3) | copy-start | bytes 4612
  14.9 2083.8 %copy-start.88 = (f32[2,192]{1,0:T(2,128)}, f32[2,192]{1,0:T(2,128)S(1)}, u32[]{:S(2)}) copy-start(f32[2,192]{1,0:T(2,128)S(1)} %fusion.188) | copy-start | bytes 4612
  17.1 2054.7 %copy-start.106 = (bf16[2,384]{1,0:T(2,128)(2,1)}, bf16[2,384]{1,0:T(2,128)(2,1)S(1)}, u32[]{:S(2)}) copy-start(bf16[2,384]{1,0:T(2,128)(2,1)S(1)} %get-tuple-element.401) | copy-start | bytes 4612
  17.2 2054.7 %copy-start.108 = (bf16[2,384]{1,0:T(2,128)(2,1)}, bf16[2,384]{1,0:T(2,128)(2,1)S(1)}, u32[]{:S(2)}) copy-start(bf16[2,384]{1,0:T(2,128)(2,1)S(1)} %get-tuple-element.402) | copy-start | bytes 4612
  17.4 2055.5 %copy-start.92 = (f32[2,768]{1,0:T(2,128)}, f32[2,768]{1,0:T(2,128)S(1)}, u32[]{:S(2)}) copy-start(f32[2,768]{1,0:T(2,128)S(1)} %select_reduce_fusion) | copy-start | bytes 18436
  17.4 80.8 %all-reduce.9.cloned.1.call-start = ((), (), s32[]{:S(2)}) async-start(), calls=%async_computation.24 | async-start | bytes 589824 | tf_op jit(solution)/shard_map/while/body/eval_jaxpr/psum | solution.py:28
  99.9 77.2 %all-reduce.9.cloned.1.call-start = ((), (), s32[]{:S(2)}) async-start(), calls=%async_computation.24 | async-start | bytes 589824 | tf_op jit(solution)/shard_map/while/body/eval_jaxpr/psum | solution.py:28
  178.8 77.2 %all-reduce.9.cloned.1.call-start = ((), (), s32[]{:S(2)}) async-start(), calls=%async_computation.24 | async-start | bytes 589824 | tf_op jit(solution)/shard_map/while/body/eval_jaxpr/psum | solution.py:28
  257.7 77.2 %all-reduce.9.cloned.1.call-start = ((), (), s32[]{:S(2)}) async-start(), calls=%async_computation.24 | async-start | bytes 589824 | tf_op jit(solution)/shard_map/while/body/eval_jaxpr/psum | solution.py:28
  336.5 77.2 %all-reduce.9.cloned.1.call-start = ((), (), s32[]{:S(2)}) async-start(), calls=%async_computation.24 | async-start | bytes 589824 | tf_op jit(solution)/shard_map/while/body/eval_jaxpr/psum | solution.py:28
  415.4 77.2 %all-reduce.9.cloned.1.call-start = ((), (), s32[]{:S(2)}) async-start(), calls=%async_computation.24 | async-start | bytes 589824 | tf_op jit(solution)/shard_map/while/body/eval_jaxpr/psum | solution.py:28
  494.3 77.2 %all-reduce.9.cloned.1.call-start = ((), (), s32[]{:S(2)}) async-start(), calls=%async_computation.24 | async-start | bytes 589824 | tf_op jit(solution)/shard_map/while/body/eval_jaxpr/psum | solution.py:28
  573.2 77.2 %all-reduce.9.cloned.1.call-start = ((), (), s32[]{:S(2)}) async-start(), calls=%async_computation.24 | async-start | bytes 589824 | tf_op jit(solution)/shard_map/while/body/eval_jaxpr/psum | solution.py:28
  652.0 77.2 %all-reduce.9.cloned.1.call-start = ((), (), s32[]{:S(2)}) async-start(), calls=%async_computation.24 | async-start | bytes 589824 | tf_op jit(solution)/shard_map/while/body/eval_jaxpr/psum | solution.py:28
  730.9 77.2 %all-reduce.9.cloned.1.call-start = ((), (), s32[]{:S(2)}) async-start(), calls=%async_computation.24 | async-start | bytes 589824 | tf_op jit(solution)/shard_map/while/body/eval_jaxpr/psum | solution.py:28
  809.8 77.2 %all-reduce.9.cloned.1.call-start = ((), (), s32[]{:S(2)}) async-start(), calls=%async_computation.24 | async-start | bytes 589824 | tf_op jit(solution)/shard_map/while/body/eval_jaxpr/psum | solution.py:28
  888.7 77.2 %all-reduce.9.cloned.1.call-start = ((), (), s32[]{:S(2)}) async-start(), calls=%async_computation.24 | async-start | bytes 589824 | tf_op jit(solution)/shard_map/while/body/eval_jaxpr/psum | solution.py:28
  967.5 77.2 %all-reduce.9.cloned.1.call-start = ((), (), s32[]{:S(2)}) async-start(), calls=%async_computation.24 | async-start | bytes 589824 | tf_op jit(solution)/shard_map/while/body/eval_jaxpr/psum | solution.py:28
  1046.4 77.2 %all-reduce.9.cloned.1.call-start = ((), (), s32[]{:S(2)}) async-start(), calls=%async_computation.24 | async-start | bytes 589824 | tf_op jit(solution)/shard_map/while/body/eval_jaxpr/psum | solution.py:28
  1125.3 77.2 %all-reduce.9.cloned.1.call-start = ((), (), s32[]{:S(2)}) async-start(), calls=%async_computation.24 | async-start | bytes 589824 | tf_op jit(solution)/shard_map/while/body/eval_jaxpr/psum | solution.py:28
  1204.1 77.2 %all-reduce.9.cloned.1.call-start = ((), (), s32[]{:S(2)}) async-start(), calls=%async_computation.24 | async-start | bytes 589824 | tf_op jit(solution)/shard_map/while/body/eval_jaxpr/psum | solution.py:28
  1283.0 77.2 %all-reduce.9.cloned.1.call-start = ((), (), s32[]{:S(2)}) async-start(), calls=%async_computation.24 | async-start | bytes 589824 | tf_op jit(solution)/shard_map/while/body/eval_jaxpr/psum | solution.py:28
  1361.9 77.2 %all-reduce.9.cloned.1.call-start = ((), (), s32[]{:S(2)}) async-start(), calls=%async_computation.24 | async-start | bytes 589824 | tf_op jit(solution)/shard_map/while/body/eval_jaxpr/psum | solution.py:28
  1440.8 77.2 %all-reduce.9.cloned.1.call-start = ((), (), s32[]{:S(2)}) async-start(), calls=%async_computation.24 | async-start | bytes 589824 | tf_op jit(solution)/shard_map/while/body/eval_jaxpr/psum | solution.py:28
  1519.7 77.2 %all-reduce.9.cloned.1.call-start = ((), (), s32[]{:S(2)}) async-start(), calls=%async_computation.24 | async-start | bytes 589824 | tf_op jit(solution)/shard_map/while/body/eval_jaxpr/psum | solution.py:28
  1598.5 77.2 %all-reduce.9.cloned.1.call-start = ((), (), s32[]{:S(2)}) async-start(), calls=%async_computation.24 | async-start | bytes 589824 | tf_op jit(solution)/shard_map/while/body/eval_jaxpr/psum | solution.py:28
  1677.4 77.2 %all-reduce.9.cloned.1.call-start = ((), (), s32[]{:S(2)}) async-start(), calls=%async_computation.24 | async-start | bytes 589824 | tf_op jit(solution)/shard_map/while/body/eval_jaxpr/psum | solution.py:28
  1756.3 77.2 %all-reduce.9.cloned.1.call-start = ((), (), s32[]{:S(2)}) async-start(), calls=%async_computation.24 | async-start | bytes 589824 | tf_op jit(solution)/shard_map/while/body/eval_jaxpr/psum | solution.py:28
  1835.2 77.2 %all-reduce.9.cloned.1.call-start = ((), (), s32[]{:S(2)}) async-start(), calls=%async_computation.24 | async-start | bytes 589824 | tf_op jit(solution)/shard_map/while/body/eval_jaxpr/psum | solution.py:28
  1914.0 77.2 %all-reduce.9.cloned.1.call-start = ((), (), s32[]{:S(2)}) async-start(), calls=%async_computation.24 | async-start | bytes 589824 | tf_op jit(solution)/shard_map/while/body/eval_jaxpr/psum | solution.py:28
  1992.9 77.2 %all-reduce.9.cloned.1.call-start = ((), (), s32[]{:S(2)}) async-start(), calls=%async_computation.24 | async-start | bytes 589824 | tf_op jit(solution)/shard_map/while/body/eval_jaxpr/psum | solution.py:28
  2071.8 51.1 %all-gather.8.cloned.1.call-start = ((), (), s32[]{:S(2)}) async-start(), calls=%async_computation.8 | async-start | bytes 2949120 | tf_op jit(solution)/shard_map/all_gather | solution.py:127
  2099.8 73.5 %reduce-scatter.13.cloned.1.call-start = ((), (), s32[]{:S(2)}) async-start(), calls=%async_computation.9 | async-start | bytes 2949120 | tf_op jit(solution)/shard_map/reduce_scatter | solution.py:131
  2101.1 21.8 copy-start.43
  2140.2 59.7 %all-gather.10.cloned.1.call-start = ((), (), s32[]{:S(2)}) async-start(), calls=%async_computation.10 | async-start | bytes 2949120 | tf_op jit(solution)/shard_map/all_gather | solution.py:127
  2141.8 34.1 copy-start.78
  2176.0 69.9 %reduce-scatter.15.cloned.1.call-start = ((), (), s32[]{:S(2)}) async-start(), calls=%async_computation.11 | async-start | bytes 2949120 | tf_op jit(solution)/shard_map/reduce_scatter | solution.py:131
  2212.9 60.9 %all-gather.12.cloned.1.call-start = ((), (), s32[]{:S(2)}) async-start(), calls=%async_computation.12 | async-start | bytes 2949120 | tf_op jit(solution)/shard_map/all_gather | solution.py:127
  2249.8 67.2 %reduce-scatter.17.cloned.1.call-start = ((), (), s32[]{:S(2)}) async-start(), calls=%async_computation.13 | async-start | bytes 2949120 | tf_op jit(solution)/shard_map/reduce_scatter | solution.py:131
  2283.8 66.3 %all-gather.14.cloned.1.call-start = ((), (), s32[]{:S(2)}) async-start(), calls=%async_computation.14 | async-start | bytes 2949120 | tf_op jit(solution)/shard_map/all_gather | solution.py:127
  2326.1 69.2 %reduce-scatter.19.cloned.1.call-start = ((), (), s32[]{:S(2)}) async-start(), calls=%async_computation.15 | async-start | bytes 2949120 | tf_op jit(solution)/shard_map/reduce_scatter | solution.py:131
  2350.2 8.7 copy-start.39
  2362.3 64.5 %all-gather.16.cloned.1.call-start = ((), (), s32[]{:S(2)}) async-start(), calls=%async_computation.16 | async-start | bytes 2949120 | tf_op jit(solution)/shard_map/all_gather | solution.py:127
  2402.7 79.4 %reduce-scatter.21.cloned.1.call-start = ((), (), s32[]{:S(2)}) async-start(), calls=%async_computation.17 | async-start | bytes 2949120 | tf_op jit(solution)/shard_map/reduce_scatter | solution.py:131
  2445.6 36.5 %copy-start.73 = (f32[2,192]{1,0:T(2,128)S(1)}, f32[2,192]{1,0:T(2,128)}, u32[]{:S(2)}) copy-start(f32[2,192]{1,0:T(2,128)} %copy-done.72) | copy-start | bytes 4612
  2449.0 65.3 %all-gather.18.cloned.1.call-start = ((), (), s32[]{:S(2)}) async-start(), calls=%async_computation.18 | async-start | bytes 2949120 | tf_op jit(solution)/shard_map/all_gather | solution.py:127
  2490.3 29.2 copy-start.21
  2490.3 29.2 copy-start.57
  2490.3 97.4 %reduce-scatter.23.cloned.1.call-start = ((), (), s32[]{:S(2)}) async-start(), calls=%async_computation.19 | async-start | bytes 2949120 | tf_op jit(solution)/shard_map/reduce_scatter | solution.py:131
  2519.5 30.1 copy-start.44
  2554.6 61.4 %reduce-scatter.25.cloned.1.call-start = ((), (), s32[]{:S(2)}) async-start(), calls=%async_computation.22 | async-start | bytes 245760
  2593.1 23.9 copy-start.81
  2596.1 44.9 %reduce-scatter.27.cloned.1.call-start = ((), (), s32[]{:S(2)}) async-start(), calls=%async_computation.23 | async-start | bytes 491520
  2597.3 22.9 copy-start.74
  2620.2 146.9 %all-reduce.7.cloned.1.call-start = ((), (), s32[]{:S(2)}) async-start(), calls=%async_computation.21 | async-start | bytes 294912 | tf_op jit(solution)/shard_map/psum | solution.py:306
  2620.9 21.1 copy-start.93
  2620.9 22.0 copy-start.107
  2620.9 719.2 %all-reduce.5.cloned.1.call-start = ((), (), s32[]{:S(2)}) async-start(), calls=%async_computation.20 | async-start | bytes 37748736 | tf_op jit(solution)/shard_map/psum | solution.py:304
  2623.9 22.3 copy-start.18
  2623.9 22.3 copy-start.23
  2768.6 625.3 %copy-start.52 = (f32[2,20,768]{2,1,0:T(8,128)S(1)}, f32[2,20,768]{2,1,0:T(8,128)}, u32[]{:S(2)}) copy-start(f32[2,20,768]{2,1,0:T(8,128)} %all-reduce.7.cloned.1.call-done) | copy-start | bytes 368644
  3340.1 57.1 %copy-start.15 = (f32[5,192,768]{2,1,0:T(8,128)S(1)}, f32[5,192,768]{2,1,0:T(8,128)}, u32[]{:S(2)}) copy-start(f32[5,192,768]{2,1,0:T(8,128)} %param.32) | copy-start | bytes 8847364
  (115 other events, 303.7 us)
Sparse Core Ops, SparseCore 0:
  24.7 73.5 all-reduce.8
  107.1 69.9 all-reduce.8
  186.0 69.9 all-reduce.8
  264.8 69.9 all-reduce.8
  343.7 69.9 all-reduce.8
  422.6 69.9 all-reduce.8
  501.5 69.9 all-reduce.8
  580.3 69.9 all-reduce.8
  659.2 69.9 all-reduce.8
  738.1 69.9 all-reduce.8
  817.0 69.9 all-reduce.8
  895.8 69.9 all-reduce.8
  974.7 69.9 all-reduce.8
  1053.6 69.9 all-reduce.8
  1132.4 69.9 all-reduce.8
  1211.3 69.9 all-reduce.8
  1290.2 69.9 all-reduce.8
  1369.1 69.9 all-reduce.8
  1448.0 69.9 all-reduce.8
  1526.9 69.9 all-reduce.8
  1605.7 69.9 all-reduce.8
  1684.6 69.9 all-reduce.8
  1763.5 69.9 all-reduce.8
  1842.4 69.9 all-reduce.8
  1921.2 69.9 all-reduce.8
  2000.1 69.9 all-reduce.8
Sparse Core Ops, SparseCore 1:
  2099.9 23.0 all-gather.7
  2140.3 32.9 reduce-scatter.12
  2176.0 23.9 all-gather.9
  2212.9 32.9 reduce-scatter.14
  2249.8 23.9 all-gather.11
  2283.9 33.0 reduce-scatter.16
  2326.2 23.9 all-gather.13
  2362.3 32.9 reduce-scatter.18
  2402.8 23.9 all-gather.15
  2449.1 33.0 reduce-scatter.20
  2490.4 23.9 all-gather.17
  2554.7 33.0 reduce-scatter.22
  2596.2 19.7 reduce-scatter.24
  2620.2 20.7 reduce-scatter.26
  2646.6 120.4 all-reduce.6
  2771.1 568.9 all-reduce.4
where the time goes:
time: 3450 us; the launch traced here: 3430 us
  waiting for transfers between devices  2770 us (80%)
  local copies, waits for them, and re-layouts  219 us (6%)
  matrix products  128 us (4%)
  loops' own time  119 us (3%)
  other arithmetic  89.9 us (3%)
  blocking collectives  76.2 us (2%)
    psum x26, waiting for transfers between devices, broadcast(): return lax.psum(jnp.where(mine, array, jnp.zeros_like(array)), axis)  1830 us
    psum x1, waiting for transfers between devices, body(): summed = lax.psum(grads, 'dp')  571 us
    all_gather x6, waiting for transfers between devices, spread(): return lax.all_gather(values, 'mp', axis=1, tiled=True)  137 us
    reduce_scatter x6, waiting for transfers between devices, collect(): lax.psum_scatter(values.astype(jnp.bfloat16), 'mp', scatter_dimension=1,...  130 us
    another operation x1, loops' own time, body(): _, fetched = lax.scan(fetch_one, 0, jnp.arange(UNITS))  118 us
    dot_general x55, matrix products, matmul(): return jnp.einsum(form, left, right, preferred_element_type=single)  107 us
    psum x1, waiting for transfers between devices, body(): lax.psum((jnp.stack([grad_in_proj, grad_out_proj]), loss_local), ('dp', '...  73.2 us
  transfers between devices with their start and end apart: 42, of which 42 were waited for; matrix products, arithmetic and copies ran while one was open for 3% of the time, Pallas kernels for 0%

commit v1 on v0

--- a/solution.py
+++ b/solution.py
@@ -25,7 +25,7 @@
 
 def broadcast(array, axis, root):
     mine = lax.axis_index(axis) == root
-    return lax.psum(jnp.where(mine, array, jnp.zeros_like(array)), axis)
+    return jnp.sum(lax.all_gather(jnp.where(mine, array, jnp.zeros_like(array)), axis), axis=0)
 
 
 def normed(values):

time: 3450 us -> 2990 us (0.87)
  waiting for transfers between devices: 2770 us -> 2270 us
  other arithmetic: 89.9 us -> 167 us
    psum x26 -> x0, waiting for transfers between devices: 1830 us -> none  [broadcast(): return lax.psum(jnp.where(mine, array, jnp.zeros_like(array)), axis)]
    all_gather x0 -> x26, waiting for transfers between devices: none -> 1320 us  [broadcast(): lax.all_gather(jnp.where(mine, array, jnp.zeros_like(array)), axis)]
    reduce_sum x0 -> x26, other arithmetic: none -> 54 us  [broadcast(): jnp.sum(lax.all_gather(jnp.where(mine, array, jnp.zeros_like(array)), axi...]
  transfers between devices with their start and end apart: 42 -> 42, of which waited for: 42 -> 42; matrix products, arithmetic and copies ran while one was open for 3% -> 4% of each run, Pallas kernels for 0% -> 0%
where the time goes in v1:
time: 2990 us; the launch traced here: 2980 us
  waiting for transfers between devices  2270 us (76%)
  local copies, waits for them, and re-layouts  195 us (7%)
  other arithmetic  167 us (6%)
  matrix products  128 us (4%)
  loops' own time  119 us (4%)
  blocking collectives  75.8 us (3%)
    all_gather x26, waiting for transfers between devices, broadcast(): lax.all_gather(jnp.where(mine, array, jnp.zeros_like(array)), axis)  1320 us
    psum x1, waiting for transfers between devices, body(): summed = lax.psum(grads, 'dp')  571 us
    all_gather x6, waiting for transfers between devices, spread(): return lax.all_gather(values, 'mp', axis=1, tiled=True)  135 us
    reduce_scatter x6, waiting for transfers between devices, collect(): lax.psum_scatter(values.astype(jnp.bfloat16), 'mp', scatter_dimension=1,...  131 us
    another operation x1, loops' own time, body(): _, fetched = lax.scan(fetch_one, 0, jnp.arange(UNITS))  118 us
    dot_general x55, matrix products, matmul(): return jnp.einsum(form, left, right, preferred_element_type=single)  107 us
    psum x1, waiting for transfers between devices, body(): lax.psum((jnp.stack([grad_in_proj, grad_out_proj]), loss_local), ('dp', '...  73.3 us
  transfers between devices with their start and end apart: 42, of which 42 were waited for; matrix products, arithmetic and copies ran while one was open for 4% of the time, Pallas kernels for 0%

profile of v1, /device:TPU:0, one launch (start us, length us, event | category | flops | bytes accessed | tf_op | source)
XLA Modules:
  0.0 2981.1 jit_solution(15505308174051827294)
XLA Ops:
  18.5 1606.0 %while.64 = (s32[]{:T(128)}, bf16[26,192,768]{2,1,0:T(8,128)(2,1)}, s32[26]{0:T(128)S(1)}, s32[26]{0:T(128)S(1)}, s32[26]{0:T(128)S(1)}, /*index=5*/bf16[5,192,7...) while((s32[]{:T(128)}, bf16[26,192,768]{2,1,0:T(8,128)(2,1)}, ...), condition=%wide.region_5.6_spmd, body=%wide.region_3.5_spmd.sunk | while | flops 1179660 | bytes 11796809 | solution.py:164
  26.6 54.9 %all-gather.21.cloned.1.call-done = bf16[8,192,768]{2,1,0:T(8,128)(2,1)} async-done(((bf16[1,192,768]{2,1,0:T(8,128)(2,1)}), bf16[8,192,768]{2,1,0:T(8,128)(2,1)}) %all-gather.21.cloned.1.call-update) | async-done | bytes 2359312 | tf_op jit(solution)/shard_map/while/body/eval_jaxpr/all_gather | solution.py:28
  92.4 50.8 %all-gather.21.cloned.1.call-done = bf16[8,192,768]{2,1,0:T(8,128)(2,1)} async-done(((bf16[1,192,768]{2,1,0:T(8,128)(2,1)}), bf16[8,192,768]{2,1,0:T(8,128)(2,1)}) %all-gather.21.cloned.1.call-update) | async-done | bytes 2359312 | tf_op jit(solution)/shard_map/while/body/eval_jaxpr/all_gather | solution.py:28
  154.0 50.8 %all-gather.21.cloned.1.call-done = bf16[8,192,768]{2,1,0:T(8,128)(2,1)} async-done(((bf16[1,192,768]{2,1,0:T(8,128)(2,1)}), bf16[8,192,768]{2,1,0:T(8,128)(2,1)}) %all-gather.21.cloned.1.call-update) | async-done | bytes 2359312 | tf_op jit(solution)/shard_map/while/body/eval_jaxpr/all_gather | solution.py:28
  215.6 50.8 %all-gather.21.cloned.1.call-done = bf16[8,192,768]{2,1,0:T(8,128)(2,1)} async-done(((bf16[1,192,768]{2,1,0:T(8,128)(2,1)}), bf16[8,192,768]{2,1,0:T(8,128)(2,1)}) %all-gather.21.cloned.1.call-update) | async-done | bytes 2359312 | tf_op jit(solution)/shard_map/while/body/eval_jaxpr/all_gather | solution.py:28
  277.2 50.8 %all-gather.21.cloned.1.call-done = bf16[8,192,768]{2,1,0:T(8,128)(2,1)} async-done(((bf16[1,192,768]{2,1,0:T(8,128)(2,1)}), bf16[8,192,768]{2,1,0:T(8,128)(2,1)}) %all-gather.21.cloned.1.call-update) | async-done | bytes 2359312 | tf_op jit(solution)/shard_map/while/body/eval_jaxpr/all_gather | solution.py:28
  338.8 50.8 %all-gather.21.cloned.1.call-done = bf16[8,192,768]{2,1,0:T(8,128)(2,1)} async-done(((bf16[1,192,768]{2,1,0:T(8,128)(2,1)}), bf16[8,192,768]{2,1,0:T(8,128)(2,1)}) %all-gather.21.cloned.1.call-update) | async-done | bytes 2359312 | tf_op jit(solution)/shard_map/while/body/eval_jaxpr/all_gather | solution.py:28
  400.4 50.8 %all-gather.21.cloned.1.call-done = bf16[8,192,768]{2,1,0:T(8,128)(2,1)} async-done(((bf16[1,192,768]{2,1,0:T(8,128)(2,1)}), bf16[8,192,768]{2,1,0:T(8,128)(2,1)}) %all-gather.21.cloned.1.call-update) | async-done | bytes 2359312 | tf_op jit(solution)/shard_map/while/body/eval_jaxpr/all_gather | solution.py:28
  462.0 50.8 %all-gather.21.cloned.1.call-done = bf16[8,192,768]{2,1,0:T(8,128)(2,1)} async-done(((bf16[1,192,768]{2,1,0:T(8,128)(2,1)}), bf16[8,192,768]{2,1,0:T(8,128)(2,1)}) %all-gather.21.cloned.1.call-update) | async-done | bytes 2359312 | tf_op jit(solution)/shard_map/while/body/eval_jaxpr/all_gather | solution.py:28
  523.6 50.8 %all-gather.21.cloned.1.call-done = bf16[8,192,768]{2,1,0:T(8,128)(2,1)} async-done(((bf16[1,192,768]{2,1,0:T(8,128)(2,1)}), bf16[8,192,768]{2,1,0:T(8,128)(2,1)}) %all-gather.21.cloned.1.call-update) | async-done | bytes 2359312 | tf_op jit(solution)/shard_map/while/body/eval_jaxpr/all_gather | solution.py:28
  585.2 50.8 %all-gather.21.cloned.1.call-done = bf16[8,192,768]{2,1,0:T(8,128)(2,1)} async-done(((bf16[1,192,768]{2,1,0:T(8,128)(2,1)}), bf16[8,192,768]{2,1,0:T(8,128)(2,1)}) %all-gather.21.cloned.1.call-update) | async-done | bytes 2359312 | tf_op jit(solution)/shard_map/while/body/eval_jaxpr/all_gather | solution.py:28
  646.8 50.8 %all-gather.21.cloned.1.call-done = bf16[8,192,768]{2,1,0:T(8,128)(2,1)} async-done(((bf16[1,192,768]{2,1,0:T(8,128)(2,1)}), bf16[8,192,768]{2,1,0:T(8,128)(2,1)}) %all-gather.21.cloned.1.call-update) | async-done | bytes 2359312 | tf_op jit(solution)/shard_map/while/body/eval_jaxpr/all_gather | solution.py:28
  708.4 50.8 %all-gather.21.cloned.1.call-done = bf16[8,192,768]{2,1,0:T(8,128)(2,1)} async-done(((bf16[1,192,768]{2,1,0:T(8,128)(2,1)}), bf16[8,192,768]{2,1,0:T(8,128)(2,1)}) %all-gather.21.cloned.1.call-update) | async-done | bytes 2359312 | tf_op jit(solution)/shard_map/while/body/eval_jaxpr/all_gather | solution.py:28
  770.0 50.8 %all-gather.21.cloned.1.call-done = bf16[8,192,768]{2,1,0:T(8,128)(2,1)} async-done(((bf16[1,192,768]{2,1,0:T(8,128)(2,1)}), bf16[8,192,768]{2,1,0:T(8,128)(2,1)}) %all-gather.21.cloned.1.call-update) | async-done | bytes 2359312 | tf_op jit(solution)/shard_map/while/body/eval_jaxpr/all_gather | solution.py:28
  831.6 50.8 %all-gather.21.cloned.1.call-done = bf16[8,192,768]{2,1,0:T(8,128)(2,1)} async-done(((bf16[1,192,768]{2,1,0:T(8,128)(2,1)}), bf16[8,192,768]{2,1,0:T(8,128)(2,1)}) %all-gather.21.cloned.1.call-update) | async-done | bytes 2359312 | tf_op jit(solution)/shard_map/while/body/eval_jaxpr/all_gather | solution.py:28
  893.2 50.8 %all-gather.21.cloned.1.call-done = bf16[8,192,768]{2,1,0:T(8,128)(2,1)} async-done(((bf16[1,192,768]{2,1,0:T(8,128)(2,1)}), bf16[8,192,768]{2,1,0:T(8,128)(2,1)}) %all-gather.21.cloned.1.call-update) | async-done | bytes 2359312 | tf_op jit(solution)/shard_map/while/body/eval_jaxpr/all_gather | solution.py:28
  954.8 50.8 %all-gather.21.cloned.1.call-done = bf16[8,192,768]{2,1,0:T(8,128)(2,1)} async-done(((bf16[1,192,768]{2,1,0:T(8,128)(2,1)}), bf16[8,192,768]{2,1,0:T(8,128)(2,1)}) %all-gather.21.cloned.1.call-update) | async-done | bytes 2359312 | tf_op jit(solution)/shard_map/while/body/eval_jaxpr/all_gather | solution.py:28
  1016.4 50.8 %all-gather.21.cloned.1.call-done = bf16[8,192,768]{2,1,0:T(8,128)(2,1)} async-done(((bf16[1,192,768]{2,1,0:T(8,128)(2,1)}), bf16[8,192,768]{2,1,0:T(8,128)(2,1)}) %all-gather.21.cloned.1.call-update) | async-done | bytes 2359312 | tf_op jit(solution)/shard_map/while/body/eval_jaxpr/all_gather | solution.py:28
  1078.1 50.8 %all-gather.21.cloned.1.call-done = bf16[8,192,768]{2,1,0:T(8,128)(2,1)} async-done(((bf16[1,192,768]{2,1,0:T(8,128)(2,1)}), bf16[8,192,768]{2,1,0:T(8,128)(2,1)}) %all-gather.21.cloned.1.call-update) | async-done | bytes 2359312 | tf_op jit(solution)/shard_map/while/body/eval_jaxpr/all_gather | solution.py:28
  1139.7 50.8 %all-gather.21.cloned.1.call-done = bf16[8,192,768]{2,1,0:T(8,128)(2,1)} async-done(((bf16[1,192,768]{2,1,0:T(8,128)(2,1)}), bf16[8,192,768]{2,1,0:T(8,128)(2,1)}) %all-gather.21.cloned.1.call-update) | async-done | bytes 2359312 | tf_op jit(solution)/shard_map/while/body/eval_jaxpr/all_gather | solution.py:28
  1201.2 50.8 %all-gather.21.cloned.1.call-done = bf16[8,192,768]{2,1,0:T(8,128)(2,1)} async-done(((bf16[1,192,768]{2,1,0:T(8,128)(2,1)}), bf16[8,192,768]{2,1,0:T(8,128)(2,1)}) %all-gather.21.cloned.1.call-update) | async-done | bytes 2359312 | tf_op jit(solution)/shard_map/while/body/eval_jaxpr/all_gather | solution.py:28
  1262.8 50.8 %all-gather.21.cloned.1.call-done = bf16[8,192,768]{2,1,0:T(8,128)(2,1)} async-done(((bf16[1,192,768]{2,1,0:T(8,128)(2,1)}), bf16[8,192,768]{2,1,0:T(8,128)(2,1)}) %all-gather.21.cloned.1.call-update) | async-done | bytes 2359312 | tf_op jit(solution)/shard_map/while/body/eval_jaxpr/all_gather | solution.py:28
  1324.5 50.8 %all-gather.21.cloned.1.call-done = bf16[8,192,768]{2,1,0:T(8,128)(2,1)} async-done(((bf16[1,192,768]{2,1,0:T(8,128)(2,1)}), bf16[8,192,768]{2,1,0:T(8,128)(2,1)}) %all-gather.21.cloned.1.call-update) | async-done | bytes 2359312 | tf_op jit(solution)/shard_map/while/body/eval_jaxpr/all_gather | solution.py:28
  1386.1 50.8 %all-gather.21.cloned.1.call-done = bf16[8,192,768]{2,1,0:T(8,128)(2,1)} async-done(((bf16[1,192,768]{2,1,0:T(8,128)(2,1)}), bf16[8,192,768]{2,1,0:T(8,128)(2,1)}) %all-gather.21.cloned.1.call-update) | async-done | bytes 2359312 | tf_op jit(solution)/shard_map/while/body/eval_jaxpr/all_gather | solution.py:28
  1447.7 50.8 %all-gather.21.cloned.1.call-done = bf16[8,192,768]{2,1,0:T(8,128)(2,1)} async-done(((bf16[1,192,768]{2,1,0:T(8,128)(2,1)}), bf16[8,192,768]{2,1,0:T(8,128)(2,1)}) %all-gather.21.cloned.1.call-update) | async-done | bytes 2359312 | tf_op jit(solution)/shard_map/while/body/eval_jaxpr/all_gather | solution.py:28
  1509.3 50.8 %all-gather.21.cloned.1.call-done = bf16[8,192,768]{2,1,0:T(8,128)(2,1)} async-done(((bf16[1,192,768]{2,1,0:T(8,128)(2,1)}), bf16[8,192,768]{2,1,0:T(8,128)(2,1)}) %all-gather.21.cloned.1.call-update) | async-done | bytes 2359312 | tf_op jit(solution)/shard_map/while/body/eval_jaxpr/all_gather | solution.py:28
  1570.9 50.8 %all-gather.21.cloned.1.call-done = bf16[8,192,768]{2,1,0:T(8,128)(2,1)} async-done(((bf16[1,192,768]{2,1,0:T(8,128)(2,1)}), bf16[8,192,768]{2,1,0:T(8,128)(2,1)}) %all-gather.21.cloned.1.call-update) | async-done | bytes 2359312 | tf_op jit(solution)/shard_map/while/body/eval_jaxpr/all_gather | solution.py:28
  1626.8 5.2 all-gather
  1634.7 8.7 all_gather.32
  1643.4 7.4 fusion.215
  1655.0 21.1 all-gather.9.cloned.1.call-done
  1680.4 9.5 while.65
  1694.8 31.7 %reduce-scatter.13.cloned.1.call-done = bf16[2,192,768]{2,1,0:T(8,128)(2,1)} async-done(((bf16[2,768,768]{2,1,0:T(8,128)(2,1)}), bf16[2,192,768]{2,1,0:T(8,128)(2,1)}) %reduce-scatter.13.cloned.1.call-update) | async-done | bytes 589840 | tf_op jit(solution)/shard_map/reduce_scatter | solution.py:131
  1731.0 22.3 all-gather.11.cloned.1.call-done
  1756.7 5.6 while.66
  1762.3 3.7 convolution_convert_fusion.6
  1769.4 29.8 reduce-scatter.15.cloned.1.call-done
  1806.5 20.6 all-gather.13.cloned.1.call-done
  1827.0 4.1 convolution_convert_fusion.5
  1832.6 4.5 convolution_convert_fusion.4
  1838.6 22.0 psum.35
  1879.8 23.6 all-gather.15.cloned.1.call-done
  1903.4 7.3 fusion.115
  1915.6 33.0 %reduce-scatter.19.cloned.1.call-done = bf16[2,192,768]{2,1,0:T(8,128)(2,1)} async-done(((bf16[2,768,768]{2,1,0:T(8,128)(2,1)}), bf16[2,192,768]{2,1,0:T(8,128)(2,1)}) %reduce-scatter.19.cloned.1.call-update) | async-done | bytes 589840 | tf_op jit(solution)/shard_map/reduce_scatter | solution.py:131
  1956.0 24.0 all-gather.17.cloned.1.call-done
  1984.2 14.6 while.67
  2002.4 32.8 %reduce-scatter.21.cloned.1.call-done = bf16[2,192,768]{2,1,0:T(8,128)(2,1)} async-done(((bf16[2,768,768]{2,1,0:T(8,128)(2,1)}), bf16[2,192,768]{2,1,0:T(8,128)(2,1)}) %reduce-scatter.21.cloned.1.call-update) | async-done | bytes 589840 | tf_op jit(solution)/shard_map/reduce_scatter | solution.py:131
  2043.5 23.9 all-gather.19.cloned.1.call-done
  2072.6 30.1 %while.68 = (s32[]{:T(128)}, bf16[2,768,3,64]{1,3,2,0:T(8,128)(2,1)}, bf16[2,768,3,64]{1,3,2,0:T(8,128)(2,1)}, bf16[2,768,3,64]{1,3,2,0:T(8,128)(2,1)}, bf16[2,7...) while((s32[]{:T(128)}, ...), condition=%wide.region_40.41_spmd, body=%wide.region_38.40_spmd.sunk | while | flops 1154430720 | bytes 65546464 | solution.py:112
  2075.1 4.5 multiply_reduce_fusion.16
  2079.7 4.5 multiply_convert_fusion.8
  2090.2 4.5 multiply_reduce_fusion.16
  2094.7 4.5 multiply_convert_fusion.8
  2102.7 4.9 convolution_convert_fusion.1
  2110.1 4.6 fusion.218
  2117.7 5.2 copy_bitcast_fusion
  2150.4 18.6 reduce-scatter.25.cloned.1.call-done
  2177.0 17.1 reduce-scatter.27.cloned.1.call-done
  2199.4 45.8 %concatenate.16 = f32[26,768,192]{1,0,2:T(8,128)} concatenate(f32[3,768,192]{1,0,2:T(4,128)S(1)} %bitcast.454, f32[1,768,192]{1,0,2:T(1,128)} %copy.315, f32[1,768,192]{1,0,2:T(1,128)} %copy.316, f32[2,768,192]{1,0,2:T(2,128)S(1)} %bitcast.470, f32[1,768,192]{1,0,2:T(1,128)} %copy.317, f32[4,768,192]{1,0,2:T(4,128)} %get-tuple-element.460, f32[4,768,192]{1,0,2:T(4,128)} %get-tuple-element.459, ...), dimensions={0} | concatenate | bytes 30670848 | tf_op jit(solution)/shard_map/concatenate | solution.py:285
  2246.8 73.3 %all-reduce.6.cloned.1.call-done = f32[2,20,768]{2,1,0:T(8,128)} async-done(((f32[2,20,768]{2,1,0:T(8,128)}), f32[2,20,768]{2,1,0:T(8,128)}) %all-reduce.6.cloned.1.call-update) | async-done | bytes 122896 | tf_op jit(solution)/shard_map/psum | solution.py:306
  2321.7 571.5 %all-reduce.4.cloned.1.call-done = f32[26,192,768]{2,0,1:T(8,128)} async-done(((f32[26,192,768]{2,0,1:T(8,128)}), f32[26,192,768]{2,0,1:T(8,128)}) %all-reduce.4.cloned.1.call-update) | async-done | bytes 15335440 | tf_op jit(solution)/shard_map/psum | solution.py:304
  2893.2 12.5 multiply_reduce_fusion.3
  2905.6 39.8 %all-reduce = (f32[]{:T(128)}, f32[]{:T(128)}) all-reduce(f32[]{:T(128)} %get-tuple-element.455, f32[]{:T(128)} %get-tuple-element.457), channel_id=1, replica_groups=mesh['dp'=8,'mp'=4] {'dp','mp'}, use_global_device_ids=true, to_apply=%region_54.55 | all-reduce | flops 2 | bytes 16 | tf_op jit(solution)/shard_map/psum | solution.py:309
  2949.2 13.9 copy_select_fusion
  (703 shorter events, 364.4 us)
Async XLA Ops:
  8.7 1617.0 %copy-start.111 = (f32[2]{0:T(128)}, f32[2]{0:T(128)S(1)}, u32[]{:S(2)}) copy-start(f32[2]{0:T(128)S(1)} %convert_element_type.204) | copy-start | bytes 28
  14.5 1712.0 %copy-start = (f32[2,192,768]{2,1,0:T(8,128)}, f32[2,192,768]{2,1,0:T(8,128)S(1)}, u32[]{:S(2)}) copy-start(f32[2,192,768]{2,1,0:T(8,128)S(1)} %get-tuple-element.453) | copy-start | bytes 3538948
  14.5 1637.9 %copy-start.76 = (f32[2,192]{1,0:T(2,128)}, f32[2,192]{1,0:T(2,128)S(1)}, u32[]{:S(2)}) copy-start(f32[2,192]{1,0:T(2,128)S(1)} %broadcast_multiply_fusion.3) | copy-start | bytes 4612
  14.9 1637.6 %copy-start.89 = (f32[2,192]{1,0:T(2,128)}, f32[2,192]{1,0:T(2,128)S(1)}, u32[]{:S(2)}) copy-start(f32[2,192]{1,0:T(2,128)S(1)} %fusion.188) | copy-start | bytes 4612
  18.2 1606.3 %copy-start.107 = (bf16[2,384]{1,0:T(2,128)(2,1)}, bf16[2,384]{1,0:T(2,128)(2,1)S(1)}, u32[]{:S(2)}) copy-start(bf16[2,384]{1,0:T(2,128)(2,1)S(1)} %get-tuple-element.446) | copy-start | bytes 4612
  18.3 1606.3 %copy-start.109 = (bf16[2,384]{1,0:T(2,128)(2,1)}, bf16[2,384]{1,0:T(2,128)(2,1)S(1)}, u32[]{:S(2)}) copy-start(bf16[2,384]{1,0:T(2,128)(2,1)S(1)} %get-tuple-element.447) | copy-start | bytes 4612
  18.5 1607.1 %copy-start.93 = (f32[2,768]{1,0:T(2,128)}, f32[2,768]{1,0:T(2,128)S(1)}, u32[]{:S(2)}) copy-start(f32[2,768]{1,0:T(2,128)S(1)} %select_reduce_fusion) | copy-start | bytes 18436
  18.5 63.0 %all-gather.21.cloned.1.call-start = ((), (), s32[]{:S(2)}) async-start(), calls=%async_computation.24 | async-start | bytes 2654208 | tf_op jit(solution)/shard_map/while/body/eval_jaxpr/all_gather | solution.py:28
  84.4 58.8 %all-gather.21.cloned.1.call-start = ((), (), s32[]{:S(2)}) async-start(), calls=%async_computation.24 | async-start | bytes 2654208 | tf_op jit(solution)/shard_map/while/body/eval_jaxpr/all_gather | solution.py:28
  146.0 58.8 %all-gather.21.cloned.1.call-start = ((), (), s32[]{:S(2)}) async-start(), calls=%async_computation.24 | async-start | bytes 2654208 | tf_op jit(solution)/shard_map/while/body/eval_jaxpr/all_gather | solution.py:28
  207.6 58.8 %all-gather.21.cloned.1.call-start = ((), (), s32[]{:S(2)}) async-start(), calls=%async_computation.24 | async-start | bytes 2654208 | tf_op jit(solution)/shard_map/while/body/eval_jaxpr/all_gather | solution.py:28
  269.1 58.8 %all-gather.21.cloned.1.call-start = ((), (), s32[]{:S(2)}) async-start(), calls=%async_computation.24 | async-start | bytes 2654208 | tf_op jit(solution)/shard_map/while/body/eval_jaxpr/all_gather | solution.py:28
  330.8 58.8 %all-gather.21.cloned.1.call-start = ((), (), s32[]{:S(2)}) async-start(), calls=%async_computation.24 | async-start | bytes 2654208 | tf_op jit(solution)/shard_map/while/body/eval_jaxpr/all_gather | solution.py:28
  392.4 58.8 %all-gather.21.cloned.1.call-start = ((), (), s32[]{:S(2)}) async-start(), calls=%async_computation.24 | async-start | bytes 2654208 | tf_op jit(solution)/shard_map/while/body/eval_jaxpr/all_gather | solution.py:28
  454.0 58.8 %all-gather.21.cloned.1.call-start = ((), (), s32[]{:S(2)}) async-start(), calls=%async_computation.24 | async-start | bytes 2654208 | tf_op jit(solution)/shard_map/while/body/eval_jaxpr/all_gather | solution.py:28
  515.6 58.8 %all-gather.21.cloned.1.call-start = ((), (), s32[]{:S(2)}) async-start(), calls=%async_computation.24 | async-start | bytes 2654208 | tf_op jit(solution)/shard_map/while/body/eval_jaxpr/all_gather | solution.py:28
  577.2 58.8 %all-gather.21.cloned.1.call-start = ((), (), s32[]{:S(2)}) async-start(), calls=%async_computation.24 | async-start | bytes 2654208 | tf_op jit(solution)/shard_map/while/body/eval_jaxpr/all_gather | solution.py:28
  638.8 58.8 %all-gather.21.cloned.1.call-start = ((), (), s32[]{:S(2)}) async-start(), calls=%async_computation.24 | async-start | bytes 2654208 | tf_op jit(solution)/shard_map/while/body/eval_jaxpr/all_gather | solution.py:28
  700.4 58.8 %all-gather.21.cloned.1.call-start = ((), (), s32[]{:S(2)}) async-start(), calls=%async_computation.24 | async-start | bytes 2654208 | tf_op jit(solution)/shard_map/while/body/eval_jaxpr/all_gather | solution.py:28
  762.0 58.8 %all-gather.21.cloned.1.call-start = ((), (), s32[]{:S(2)}) async-start(), calls=%async_computation.24 | async-start | bytes 2654208 | tf_op jit(solution)/shard_map/while/body/eval_jaxpr/all_gather | solution.py:28
  823.6 58.8 %all-gather.21.cloned.1.call-start = ((), (), s32[]{:S(2)}) async-start(), calls=%async_computation.24 | async-start | bytes 2654208 | tf_op jit(solution)/shard_map/while/body/eval_jaxpr/all_gather | solution.py:28
  885.2 58.8 %all-gather.21.cloned.1.call-start = ((), (), s32[]{:S(2)}) async-start(), calls=%async_computation.24 | async-start | bytes 2654208 | tf_op jit(solution)/shard_map/while/body/eval_jaxpr/all_gather | solution.py:28
  946.8 58.8 %all-gather.21.cloned.1.call-start = ((), (), s32[]{:S(2)}) async-start(), calls=%async_computation.24 | async-start | bytes 2654208 | tf_op jit(solution)/shard_map/while/body/eval_jaxpr/all_gather | solution.py:28
  1008.4 58.8 %all-gather.21.cloned.1.call-start = ((), (), s32[]{:S(2)}) async-start(), calls=%async_computation.24 | async-start | bytes 2654208 | tf_op jit(solution)/shard_map/while/body/eval_jaxpr/all_gather | solution.py:28
  1070.0 58.8 %all-gather.21.cloned.1.call-start = ((), (), s32[]{:S(2)}) async-start(), calls=%async_computation.24 | async-start | bytes 2654208 | tf_op jit(solution)/shard_map/while/body/eval_jaxpr/all_gather | solution.py:28
  1131.6 58.8 %all-gather.21.cloned.1.call-start = ((), (), s32[]{:S(2)}) async-start(), calls=%async_computation.24 | async-start | bytes 2654208 | tf_op jit(solution)/shard_map/while/body/eval_jaxpr/all_gather | solution.py:28
  1193.2 58.8 %all-gather.21.cloned.1.call-start = ((), (), s32[]{:S(2)}) async-start(), calls=%async_computation.24 | async-start | bytes 2654208 | tf_op jit(solution)/shard_map/while/body/eval_jaxpr/all_gather | solution.py:28
  1254.8 58.8 %all-gather.21.cloned.1.call-start = ((), (), s32[]{:S(2)}) async-start(), calls=%async_computation.24 | async-start | bytes 2654208 | tf_op jit(solution)/shard_map/while/body/eval_jaxpr/all_gather | solution.py:28
  1316.4 58.8 %all-gather.21.cloned.1.call-start = ((), (), s32[]{:S(2)}) async-start(), calls=%async_computation.24 | async-start | bytes 2654208 | tf_op jit(solution)/shard_map/while/body/eval_jaxpr/all_gather | solution.py:28
  1378.0 58.8 %all-gather.21.cloned.1.call-start = ((), (), s32[]{:S(2)}) async-start(), calls=%async_computation.24 | async-start | bytes 2654208 | tf_op jit(solution)/shard_map/while/body/eval_jaxpr/all_gather | solution.py:28
  1439.7 58.8 %all-gather.21.cloned.1.call-start = ((), (), s32[]{:S(2)}) async-start(), calls=%async_computation.24 | async-start | bytes 2654208 | tf_op jit(solution)/shard_map/while/body/eval_jaxpr/all_gather | solution.py:28
  1501.2 58.8 %all-gather.21.cloned.1.call-start = ((), (), s32[]{:S(2)}) async-start(), calls=%async_computation.24 | async-start | bytes 2654208 | tf_op jit(solution)/shard_map/while/body/eval_jaxpr/all_gather | solution.py:28
  1562.9 58.8 %all-gather.21.cloned.1.call-start = ((), (), s32[]{:S(2)}) async-start(), calls=%async_computation.24 | async-start | bytes 2654208 | tf_op jit(solution)/shard_map/while/body/eval_jaxpr/all_gather | solution.py:28
  1624.5 51.6 %all-gather.9.cloned.1.call-start = ((), (), s32[]{:S(2)}) async-start(), calls=%async_computation.8 | async-start | bytes 2949120 | tf_op jit(solution)/shard_map/all_gather | solution.py:127
  1653.6 73.0 %reduce-scatter.13.cloned.1.call-start = ((), (), s32[]{:S(2)}) async-start(), calls=%async_computation.9 | async-start | bytes 2949120 | tf_op jit(solution)/shard_map/reduce_scatter | solution.py:131
  1655.0 21.1 copy-start.42
  1693.5 59.8 %all-gather.11.cloned.1.call-start = ((), (), s32[]{:S(2)}) async-start(), calls=%async_computation.10 | async-start | bytes 2949120 | tf_op jit(solution)/shard_map/all_gather | solution.py:127
  1694.8 34.4 %copy-start.79 = (f32[2,1,768]{2,0,1:T(2,128)}, f32[2,1,768]{2,0,1:T(2,128)S(1)}, u32[]{:S(2)}) copy-start(f32[2,1,768]{2,0,1:T(2,128)S(1)} %copy.295) | copy-start | bytes 18436
  1729.2 69.9 %reduce-scatter.15.cloned.1.call-start = ((), (), s32[]{:S(2)}) async-start(), calls=%async_computation.11 | async-start | bytes 2949120 | tf_op jit(solution)/shard_map/reduce_scatter | solution.py:131
  1766.1 60.9 %all-gather.13.cloned.1.call-start = ((), (), s32[]{:S(2)}) async-start(), calls=%async_computation.12 | async-start | bytes 2949120 | tf_op jit(solution)/shard_map/all_gather | solution.py:127
  1803.0 67.1 %reduce-scatter.17.cloned.1.call-start = ((), (), s32[]{:S(2)}) async-start(), calls=%async_computation.13 | async-start | bytes 2949120 | tf_op jit(solution)/shard_map/reduce_scatter | solution.py:131
  1837.1 66.3 %all-gather.15.cloned.1.call-start = ((), (), s32[]{:S(2)}) async-start(), calls=%async_computation.14 | async-start | bytes 2949120 | tf_op jit(solution)/shard_map/all_gather | solution.py:127
  1879.4 69.2 %reduce-scatter.19.cloned.1.call-start = ((), (), s32[]{:S(2)}) async-start(), calls=%async_computation.15 | async-start | bytes 2949120 | tf_op jit(solution)/shard_map/reduce_scatter | solution.py:131
  1915.5 64.4 %all-gather.17.cloned.1.call-start = ((), (), s32[]{:S(2)}) async-start(), calls=%async_computation.16 | async-start | bytes 2949120 | tf_op jit(solution)/shard_map/all_gather | solution.py:127
  1955.9 79.4 %reduce-scatter.21.cloned.1.call-start = ((), (), s32[]{:S(2)}) async-start(), calls=%async_computation.17 | async-start | bytes 2949120 | tf_op jit(solution)/shard_map/reduce_scatter | solution.py:131
  1998.8 36.5 %copy-start.75 = (f32[2,192]{1,0:T(2,128)S(1)}, f32[2,192]{1,0:T(2,128)}, u32[]{:S(2)}) copy-start(f32[2,192]{1,0:T(2,128)} %copy-done.74) | copy-start | bytes 4612
  2002.2 65.2 %all-gather.19.cloned.1.call-start = ((), (), s32[]{:S(2)}) async-start(), calls=%async_computation.18 | async-start | bytes 2949120 | tf_op jit(solution)/shard_map/all_gather | solution.py:127
  2043.4 29.2 copy-start.20
  2043.4 29.2 copy-start.57
  2043.4 97.3 %reduce-scatter.23.cloned.1.call-start = ((), (), s32[]{:S(2)}) async-start(), calls=%async_computation.19 | async-start | bytes 2949120 | tf_op jit(solution)/shard_map/reduce_scatter | solution.py:131
  2072.6 30.1 %copy-start.43 = (bf16[3,768,192]{1,2,0:T(8,128)(2,1)S(1)}, bf16[3,768,192]{1,2,0:T(8,128)(2,1)}, u32[]{:S(2)}) copy-start(bf16[3,768,192]{1,2,0:T(8,128)(2,1)} %copy-done.42) | copy-start | bytes 2654212
  2107.7 61.3 %reduce-scatter.25.cloned.1.call-start = ((), (), s32[]{:S(2)}) async-start(), calls=%async_computation.22 | async-start | bytes 245760
  2146.2 23.9 copy-start.82
  2149.2 44.8 %reduce-scatter.27.cloned.1.call-start = ((), (), s32[]{:S(2)}) async-start(), calls=%async_computation.23 | async-start | bytes 491520
  2173.2 146.9 %all-reduce.6.cloned.1.call-start = ((), (), s32[]{:S(2)}) async-start(), calls=%async_computation.21 | async-start | bytes 294912 | tf_op jit(solution)/shard_map/psum | solution.py:306
  2174.0 21.1 copy-start.94
  2174.0 22.0 copy-start.108
  2174.0 719.2 %all-reduce.4.cloned.1.call-start = ((), (), s32[]{:S(2)}) async-start(), calls=%async_computation.20 | async-start | bytes 37748736 | tf_op jit(solution)/shard_map/psum | solution.py:304
  2177.0 22.4 copy-start.17
  2177.0 22.4 copy-start.22
  2321.7 625.2 %copy-start.51 = (f32[2,20,768]{2,1,0:T(8,128)S(1)}, f32[2,20,768]{2,1,0:T(8,128)}, u32[]{:S(2)}) copy-start(f32[2,20,768]{2,1,0:T(8,128)} %all-reduce.6.cloned.1.call-done) | copy-start | bytes 368644
  2321.7 625.2 %copy-start.52 = (f32[2,20,768]{2,0,1:T(2,128)S(1)}, f32[2,20,768]{2,0,1:T(2,128)}, u32[]{:S(2)}) copy-start(f32[2,20,768]{2,0,1:T(2,128)} %param.35) | copy-start | bytes 368644
  2321.7 625.2 %copy-start.70 = (f32[2,20,768]{2,0,1:T(2,128)S(1)}, f32[2,20,768]{2,0,1:T(2,128)}, u32[]{:S(2)}) copy-start(f32[2,20,768]{2,0,1:T(2,128)} %param.37) | copy-start | bytes 368644
  2321.7 625.2 %copy-start.71 = (f32[2,20,768]{2,0,1:T(2,128)S(1)}, f32[2,20,768]{2,0,1:T(2,128)}, u32[]{:S(2)}) copy-start(f32[2,20,768]{2,0,1:T(2,128)} %param.36) | copy-start | bytes 368644
  (116 other events, 323.1 us)
Sparse Core Ops, SparseCore 0:
  26.7 54.7 all-gather.20
  92.5 50.5 all-gather.20
  154.1 50.5 all-gather.20
  215.7 50.5 all-gather.20
  277.3 50.5 all-gather.20
  338.9 50.5 all-gather.20
  400.5 50.5 all-gather.20
  462.1 50.5 all-gather.20
  523.7 50.5 all-gather.20
  585.3 50.5 all-gather.20
  646.9 50.5 all-gather.20
  708.5 50.5 all-gather.20
  770.1 50.5 all-gather.20
  831.7 50.5 all-gather.20
  893.3 50.5 all-gather.20
  954.9 50.5 all-gather.20
  1016.6 50.5 all-gather.20
  1078.2 50.5 all-gather.20
  1139.8 50.5 all-gather.20
  1201.4 50.5 all-gather.20
  1263.0 50.5 all-gather.20
  1324.6 50.5 all-gather.20
  1386.2 50.5 all-gather.20
  1447.8 50.5 all-gather.20
  1509.4 50.5 all-gather.20
  1571.0 50.5 all-gather.20
Sparse Core Ops, SparseCore 1:
  1653.6 22.4 all-gather.8
  1693.5 33.0 reduce-scatter.12
  1729.3 23.9 all-gather.10
  1766.2 33.0 reduce-scatter.14
  1803.1 23.9 all-gather.12
  1837.2 32.9 reduce-scatter.16
  1879.4 23.9 all-gather.14
  1915.6 33.0 reduce-scatter.18
  1956.0 23.9 all-gather.16
  2002.3 32.9 reduce-scatter.20
  2043.5 23.9 all-gather.18
  2107.8 33.0 reduce-scatter.22
  2149.3 19.6 reduce-scatter.24
  2173.3 20.7 reduce-scatter.26
  2199.6 120.5 all-reduce.5
  2324.2 568.9 all-reduce.3
